TPU v7x, 32 devices: a whole 2x2x4 slice. The times are simulated.
32 devices in a mesh: dp: 8 (over z, y), section: 4 (over x, core).
Axes of the slice: x: 2, y: 2, z: 4, core: 2. Of those that a mesh axis runs over, the one named last changes fastest.
Arguments:
- field_inputs: float32 [4096, 8, 256], P('dp', 'section'), may hold values from -6 to 6
- field_weight: float32 [8], P('section'), may hold values from 0.2 to 2
- norm_gain: float32 [256], replicated, may hold values from 0.1 to 1.9
- gate_weight: float32 [2, 256, 80], replicated, may hold values from -0.375 to 0.375
- expert_in: float32 [32, 256, 256], P('section'), may hold values from -0.375 to 0.375
- expert_out: float32 [32, 256, 256], P('section'), may hold values from -2 to 2
- tower_in: float32 [4, 256, 128], P('section'), may hold values from -0.375 to 0.375
- tower_out: float32 [4, 128], P('section'), may hold values from -0.5 to 0.5
- tower_bias: float32 [4], P('section'), may hold values from -4 to 4
- labels: float32 [4096, 4], P('dp', 'section'), may hold values from 0 to 1
- source_ids: int32 [4096], P('dp'), may hold values from 0 to 31, as said below
- task_table: int32 [32, 4], P(None, 'section'), may hold values from 0 to 1, as said below
Outputs:
- predictions: float32 [4096, 4], P('dp', 'section')
- inputs_grad: float32 [4096, 8, 256], P('dp', 'section')
- field_weight_grad: float32 [8], P('section')
- norm_gain_grad: float32 [256], replicated
- gate_weight_grad: float32 [2, 256, 80], replicated
- expert_in_grad: float32 [32, 256, 256], P('section')
- expert_out_grad: float32 [32, 256, 256], P('section')
- tower_in_grad: float32 [4, 256, 128], P('section')
- tower_out_grad: float32 [4, 128], P('section')
- tower_bias_grad: float32 [4], P('section')
Inputs may be any that keep to these rules, and one draw needn't show every extreme that they name: `source_ids`: row 0 has source 0 and the last row source 32 - 1. `task_table`: source s labels exactly 1 + (s mod 4) of the 4 tasks.
All inputs are finite; a program needn't handle non-finite values.
Results may differ from a plain program's by a relative error of at most 0.0003.
Values sent between devices are 32-bit elements; how exact they have to be, the bound alone decides.
A program may use at most 256 MiB of HBM per device.

v0:
```python
from functools import partial

import jax
import jax.numpy as jnp
from jax import lax
from jax.experimental import pallas as pl
from jax.experimental.pallas import tpu as pltpu
from jax.sharding import PartitionSpec as P

D = 256
H = 256
E = 16
TASKS = 4
SEL = 4
BITS = 4
TOWER = 128
SOURCES = 32
HALF = E // 2
GROWS = 32
FROWS = 96

STEP_SLOPE = 0.6
ENTROPY_WEIGHT = 0.05
NORM_EPS = 1e-05
GELU_A = 0.7978845608028654
GELU_B = 0.044715

F32 = jnp.float32
BF16 = jnp.bfloat16
MESH = pl.DeviceIdType.MESH

K_W, K_P, K_SM, K_TI, K_UP, K_DOWN, K_TW, K_DG, K_DP, K_GO, K_DX = 0, 2, 4, 8, 12, 16, 20, 24, 25, 28, 32
K_COUNT = 48
TILE = 32
SPILL = TASKS - 1
AHEAD = 3

GATE_AT = TOWER
MISC_AT = GATE_AT + 2 * GROWS
SMALL = MISC_AT + 8
KEPT = SMALL - GATE_AT


def split(x):
    hi = x.astype(BF16)
    return hi, (x - hi.astype(F32)).astype(BF16)


def wide(x):
    hi, lo = split(x)
    return jnp.concatenate([hi, lo, hi], axis=1)


def tall(x):
    hi, lo = split(x)
    return jnp.concatenate([hi, hi, lo], axis=0)


def put(ref, at, x):
    k = x.shape[1]
    hi, lo = split(x)
    ref[*at, :k] = hi
    ref[*at, k:] = lo


def stack(x):
    k = x.shape[1] // 2
    return jnp.concatenate([x[:, :k], x[:, :k], x[:, k:]], axis=0)


def mm(a, b):
    return jnp.dot(a, b, preferred_element_type=F32)


def pair(x):
    k = x.shape[1] // 2
    return jnp.concatenate([x, x[:, :k]], axis=1)


def gelu_pair(x):
    x2 = x * x
    h = 0.5 + 0.5 * jnp.tanh(x * (GELU_A + (GELU_A * GELU_B) * x2))
    g = x * h
    slope = h + g * (1.0 - h) * (2.0 * GELU_A + (6.0 * GELU_A * GELU_B) * x2)
    return g, slope


def rows8(x):
    return jnp.sum(x.reshape(x.shape[0] // 8, 8, x.shape[1]), axis=0)


def over_selectors(v, groups, op):
    parts = [v[k * groups : (k + 1) * groups] for k in range(SEL)]
    return op(op(parts[0], parts[1]), op(parts[2], parts[3]))


def to_selectors(v):
    return jnp.concatenate([v] * SEL, axis=0)


def gate_state(c, groups):
    w = SEL * groups
    zs = [c[w * b : w * b + w] * STEP_SLOPE for b in range(BITS)]
    alpha = c[w * BITS : w * BITS + w]
    ups, downs, sig_p, sig_n = [], [], [], []
    for z in zs:
        e = jnp.exp(-jnp.abs(z))
        tail = jnp.log1p(e)
        ups.append(jnp.minimum(z, 0.0) - tail)
        downs.append(jnp.minimum(-z, 0.0) - tail)
        big = 1.0 / (1.0 + e)
        small = e * big
        sig_p.append(jnp.where(z >= 0.0, big, small))
        sig_n.append(jnp.where(z >= 0.0, small, big))
    low = [(ups[0] if k & 1 else downs[0]) + (ups[1] if k & 2 else downs[1]) for k in range(4)]
    high = [(ups[2] if k & 1 else downs[2]) + (ups[3] if k & 2 else downs[3]) for k in range(4)]
    log_r = [low[j & 3] + high[j >> 2] for j in range(E)]
    r = [jnp.exp(v) for v in log_r]
    top = jnp.exp(alpha - to_selectors(over_selectors(alpha, groups, jnp.maximum)))
    mix = top / to_selectors(over_selectors(top, groups, jnp.add))
    return log_r, r, mix, sig_p, sig_n


def gate_forward(c, groups):
    _, r, mix, _, _ = gate_state(c, groups)
    return [over_selectors(mix * v, groups, jnp.add) for v in r]


def gate_backward(c, dgate, groups, out):
    log_r, r, mix, sig_p, sig_n = gate_state(c, groups)
    yield
    total = jnp.zeros_like(mix)
    on = [jnp.zeros_like(mix) for _ in range(BITS)]
    off = [jnp.zeros_like(mix) for _ in range(BITS)]
    for j in range(E):
        dg = to_selectors(dgate(j))
        total = total + dg * r[j]
        dlog = r[j] * (mix * dg - ENTROPY_WEIGHT * (log_r[j] + 1.0))
        for b in range(BITS):
            if j >> b & 1:
                on[b] = on[b] + dlog
            else:
                off[b] = off[b] + dlog
        yield
    dalpha = mix * (total - to_selectors(over_selectors(mix * total, groups, jnp.add)))
    dz = [STEP_SLOPE * (on[b] * sig_n[b] - off[b] * sig_p[b]) for b in range(BITS)]
    used = SEL * (BITS + 1) * groups
    pad = jnp.zeros(((-used) % GROWS, c.shape[1]), F32)
    out.append(jnp.concatenate(dz + [dalpha, pad], axis=0))
    yield


def t_dot(a, b):
    ah, al = split(a)
    left = jnp.concatenate([ah, al, ah], axis=0)
    return lax.dot_general(left, tall(b), (((0,), (0,)), ((), ())), preferred_element_type=F32)


def weave(count, first, middle, last, extra=()):
    extra = iter(extra)
    for step in range(count + 2):
        if step < count:
            first(step, step % 2)
        next(extra, None)
        if 0 <= step - 1 < count:
            middle(step - 1, (step - 1) % 2, 0)
        next(extra, None)
        if step >= 2:
            last(step - 2, step % 2)
        next(extra, None)
        if 0 <= step - 1 < count:
            middle(step - 1, (step - 1) % 2, 1)
        next(extra, None)
    for _ in extra:
        pass


def halves(size):
    tiles = [slice(a, a + TILE) for a in range(0, size, TILE)]
    return tiles[: len(tiles) // 2], tiles[len(tiles) // 2 :]


def kernel(
    n,
    subs,
    small_rows,
    x_ref,
    fw_ref,
    gain_ref,
    gate_ref,
    win_ref,
    wout_ref,
    tin_ref,
    tout_ref,
    tbias_ref,
    labels_ref,
    ids_ref,
    table_ref,
    o_pred,
    o_ig,
    o_fw,
    o_gain,
    o_gate,
    o_in,
    o_out,
    o_tin,
    o_tout,
    o_bias,
    kept,
    wt,
    w_in,
    w_out,
    a1,
    a2,
    d_in,
    d_out,
    gbuf,
    kbuf,
    kp,
    rd,
    xf,
    part,
    pre0,
    pre1,
    pre2,
    pre,
    inbox,
    outbox,
    u_t,
    u_n,
    s_t,
    s_n,
    bb,
    acc,
    wg,
    gt,
    gt0,
    cs,
    dgt,
    dg,
    gb,
    sm,
    smo,
    ti,
    tp,
    tw,
    dp,
    gain_row,
    columns,
    u_next,
    gt_next,
    cs_next,
    acc_b,
    dy_kept,
    held,
    tm,
    sb,
    sr,
    so,
    sa,
    sg,
    send,
    recv,
    local,
    fetch_sem,
    ready,
    rs_send,
    rs_recv,
    ag_send,
    ag_recv,
    store_sem,
    sr_send,
    sr_recv,
    sa_send,
    sa_recv,
):
    s = lax.axis_index("section")
    x = s // 2
    c = s % 2
    mate = s + 1 - 2 * c
    across = s + 2 - 4 * x
    diag = 3 - s
    R = part.shape[0] // 2
    mine = pl.ds(pl.multiple_of(c * R, R), R)
    theirs = pl.ds(pl.multiple_of((1 - c) * R, R), R)

    me = lax.axis_index("dp")
    odd = me % 2
    p = (1 - odd) * (me // 2) + odd * (n - 1 - me // 2)

    def ring_id(q):
        far = q // (n // 2)
        return (1 - far) * 2 * q + far * (2 * (n - 1 - q) + 1)

    nbr = [ring_id((p + 1) % n), ring_id((p + n - 1) % n)]

    barrier = pltpu.get_barrier_semaphore()
    for sec in (mate, across, diag):
        pl.semaphore_signal(barrier, inc=1, device_id={"section": sec}, device_id_type=MESH)

    def greet(i, carry):
        pl.semaphore_signal(barrier, inc=1, device_id={"dp": (me + i) % n}, device_id_type=MESH)
        return carry

    lax.fori_loop(1, n, greet, 0)
    fields = [pltpu.make_async_copy(x_ref.at[:, f], xf.at[f], local.at[2 + f]) for f in range(2)]
    for f in fields:
        f.start()
    own = pl.ds(pl.multiple_of(c * HALF * H, HALF * H), HALF * H)
    own_in = pltpu.make_async_copy(win_ref, d_in.at[own], local.at[0])
    own_out = pltpu.make_async_copy(wout_ref, d_out.at[own], local.at[1])
    own_in.start()
    own_out.start()
    pl.semaphore_wait(barrier, 3 + n - 1)

    def copy(src, dst, k, sec, ks=None):
        return pltpu.make_async_remote_copy(
            src_ref=src,
            dst_ref=dst,
            send_sem=send.at[k if ks is None else ks],
            recv_sem=recv.at[k],
            device_id={"section": sec},
            device_id_type=MESH,
        )

    def expert(j, count=1):
        return pl.ds(pl.multiple_of(j * H, H), count * H)

    for f in fields:
        f.wait()
    part[...] = xf[0] * fw_ref[0, 0] + xf[1] * fw_ref[0, 1]
    to_mate = copy(part.at[theirs], pre0, K_P, mate)
    to_mate.start()
    swap_in = copy(d_in.at[own], d_in.at[own], K_W, mate)
    swap_out = copy(d_out.at[own], d_out.at[own], K_W + 1, mate)
    own_in.wait()
    swap_in.start()
    own_out.wait()
    swap_out.start()

    ids = ids_ref[...]
    mask = jnp.zeros(ids.shape, F32)
    for q in range(SOURCES):
        mask = mask + jnp.where(ids == q, table_ref[0, q].astype(F32), 0.0)
    smo[...] = jnp.zeros_like(smo)
    smo[0:1] = labels_ref[...]
    smo[1:2] = mask
    smo[2:3, :TOWER] = tout_ref[...]
    smo[3:4] = jnp.zeros((1, 2 * R), F32) + tbias_ref[0, 0]
    for k in range(2):

        @pl.when(s != 2 + k)
        def _():
            copy(smo, sm.at[s], K_SM + s, 2 + k, K_SM + k).start()
            copy(tin_ref, ti.at[s], K_TI + s, 2 + k, K_TI + k).start()

    to_mate.wait_recv()

    @pl.when(x == 1)
    def _():
        pre2[...] = part[mine] + pre0[...]
        copy(pre2, pre1, K_P + 1, across).start()
        sm[s] = smo[...]
        ti[s] = tin_ref[...]

    wg[...] = jnp.zeros_like(wg)

    @pl.when(x == 0)
    def _():
        def order(t, carry):
            for sel in range(SEL):
                for e in range(BITS + 1):
                    row = t * (SEL * (BITS + 1)) + sel * (BITS + 1) + e
                    wg[pl.ds((e * SEL + sel) * TASKS + t, 1)] = gate_ref[0, pl.ds(row, 1)]
            return carry

        lax.fori_loop(0, TASKS, order, 0)

    @pl.when(x == 1)
    def _():
        def order(t, carry):
            for sel in range(SEL):
                for e in range(BITS + 1):
                    row = t * (SEL * (BITS + 1)) + sel * (BITS + 1) + e
                    wg[pl.ds(t * GROWS + e * SEL + sel, 1)] = gate_ref[1, pl.ds(row, 1)]
            return carry

        lax.fori_loop(0, TASKS, order, 0)

    def keep_plain(e, carry):
        put(w_in.at[e], (slice(None),), d_in[expert(e)])
        put(w_out.at[e], (slice(None),), d_out[expert(e)])
        return carry

    def keep_flipped(e, carry):
        put(wt.at[e], (slice(None),), d_in[expert(e)].T)
        put(wt.at[E + e], (slice(None),), d_out[expert(e)].T)
        return carry

    lax.fori_loop(c * HALF, c * HALF + HALF, keep_plain, 0)
    swap_in.wait()
    swap_out.wait()
    lax.fori_loop((1 - c) * HALF, (1 - c) * HALF + HALF, keep_plain, 0)

    def rows_of(size):
        return [slice(a, a + TILE) for a in range(0, size, TILE)]

    def shifted(tile, e):
        return slice(e * H + tile.start, e * H + tile.stop)

    chunk = HALF * H // n
    sub = chunk // subs
    lanes = [(d, k) for d in range(2) for k in range(subs)]

    def at(k, q):
        return pl.ds(pl.multiple_of(q * chunk + k * sub, 8), sub)

    def holds(d, step):
        return (p + n - step) % n if d == 0 else (p + step) % n

    def slot(d, k, step):
        return pl.ds(pl.multiple_of(((d * subs + k) * (n - 1) + step) * sub, 8), sub)

    def rs(d, k, step, src):
        return pltpu.make_async_remote_copy(
            src_ref=src,
            dst_ref=a1.at[slot(d, k, step)],
            send_sem=rs_send.at[d, k, step],
            recv_sem=rs_recv.at[d, k, step],
            device_id={"dp": nbr[d]},
            device_id_type=MESH,
        )

    results = (o_in, o_out)

    def landed(d, k, q):
        return a2.at[pl.ds(pl.multiple_of(d * HALF * H + q * chunk + k * sub, 8), sub)]

    def store(d, k, q, src, step):
        return pltpu.make_async_copy(src, results[d].at[at(k, q)], store_sem.at[d, k, step])

    def ag(d, k, step, src, q):
        return pltpu.make_async_remote_copy(
            src_ref=src,
            dst_ref=landed(d, k, q),
            send_sem=ag_send.at[d, k, step],
            recv_sem=ag_recv.at[d, k, step],
            device_id={"dp": nbr[d]},
            device_id_type=MESH,
        )

    def give(e):
        j = (1 - c) * HALF + e
        return (
            copy(d_in.at[expert(j)], rd.at[0, expert(e)], K_DX + e, mate),
            copy(d_out.at[expert(j)], rd.at[1, expert(e)], K_DX + HALF + e, mate),
        )

    start_at = p * chunk // H

    def near(k):
        return (start_at + HALF + ((k + 1) // 2) * (1 - 2 * (k % 2))) % HALF

    def turn_of(i):
        own_turn = i % 2
        return ((1 - own_turn) * (1 - c) + own_turn * c) * HALF + near(i // 2)

    def fetch(i):
        at = pl.ds((i % (AHEAD + 1)) * 8, 2 * SPILL)
        return pltpu.make_async_copy(kept.at[turn_of(i)], wt.at[at], fetch_sem.at[i % (AHEAD + 1)])

    def fetch_start(i):
        for k in range(2 * SPILL):
            slab = (i % (AHEAD + 1)) * 8 + k
            pltpu.make_async_copy(
                kept.at[turn_of(i), k], wt.at[slab], fetch_sem.at[i % (AHEAD + 1)]
            ).start()

    def greet_ring():
        for dev in nbr:
            pl.semaphore_signal(ready, inc=1, device_id={"dp": dev}, device_id_type=MESH)

    def merge(k, carry):
        e = near(k)
        for move in give(e):
            move.wait_recv()
        rows = expert(e)
        rd[0, rows] = (rd[0, rows] + d_in[expert(c * HALF + e)]).T
        rd[1, rows] += d_out[expert(c * HALF + e)]
        return carry

    def ring_start():
        pl.semaphore_wait(ready, 2)
        for d, k in lanes:
            rs(d, k, 0, rd.at[d, at(k, holds(d, 0))]).start()

    def reduce_step(step, carry):
        for d, k in lanes:
            rs(d, k, step - 1, a1.at[slot(d, k, step - 1)]).wait_recv()
            a1[slot(d, k, step - 1)] += rd[d, at(k, holds(d, step))]
            rs(d, k, step, a1.at[slot(d, k, step - 1)]).start()
        return carry

    @pl.when(x == 0)
    def _():
        copy(pre2, pre1, K_P + 1, across).wait_recv()
        pre_rows = part[mine] + pre0[...] + pre1[...]
        pre[...] = pre_rows
        rho = lax.rsqrt(jnp.mean(pre_rows * pre_rows, axis=1, keepdims=True) + NORM_EPS)
        pooled = pre_rows * rho * gain_ref[...]
        acc[...] = pooled
        u_n[0] = tall(pooled)
        u_t[...] = tall(pooled.T)
        logits = mm(wide(wg[:FROWS]), u_t[...])
        cs[...] = logits
        gates = gate_forward(logits, TASKS)
        for j, g in enumerate(gates):
            gt0[j] = g

        def first(j, par):
            left = jnp.concatenate([u_n[0, :R], u_n[0, 2 * R :], u_n[0, :R]], axis=1)
            bb[par] = mm(left, stack(w_in[j]))

        def activate(j, par, part_no):
            for tile in halves(R)[part_no]:
                value, slope = gelu_pair(bb[par, tile])
                a1[shifted(tile, j)] = value
                a2[shifted(tile, j)] = slope
                put(gbuf, (j, tile), value)

        def finish(j, par):
            d_in[expert(j)] = mm(pair(gbuf[j]), stack(w_out[j]))

        weave(E, first, activate, finish)
        columns[...] = jnp.concatenate(gates, axis=0).T

        for t in range(TASKS):

            def mix(i, carry):
                tile = pl.ds(pl.multiple_of(i * TILE, TILE), TILE)
                cols = columns[tile]
                total = acc[tile]
                for j in range(E):
                    rows = pl.ds(pl.multiple_of(j * R + i * TILE, TILE), TILE)
                    total = total + cols[:, j * TASKS + t : j * TASKS + t + 1] * d_in[rows]
                outbox[t, tile] = total
                return carry

            lax.fori_loop(0, R // TILE, mix, 0)
            copy(outbox.at[t], inbox.at[t], K_UP + t, across).start()

        def flip(j, carry):
            value = a1[expert(j)].T
            a1[expert(j)] = value
            put(gbuf.at[j], (slice(None),), value)
            a2[expert(j)] = a2[expert(j)].T
            d_in[expert(j)] = d_in[expert(j)].T
            return carry

        lax.fori_loop(0, E, flip, 0)
        greet_ring()
        d_out[...] = jnp.zeros_like(d_out)
        acc[...] = jnp.zeros_like(acc)

    @pl.when(x == 1)
    def _():
        lax.fori_loop(0, E, keep_flipped, 0)
        for q in range(TASKS):

            @pl.when(s != q)
            def _():
                copy(smo, sm.at[q], K_SM + q, q).wait_recv()
                copy(tin_ref, ti.at[q], K_TI + q, q).wait_recv()

        def keep(k, t):
            return pltpu.make_async_copy((gbuf, kbuf)[k], kept.at[:, k * SPILL + t], local.at[4 + k])

        def keep_start(k, t):
            def one(j, carry):
                pltpu.make_async_copy((gbuf, kbuf)[k].at[j], kept.at[j, k * SPILL + t], local.at[4 + k]).start()
                return carry

            @pl.when(t < SPILL)
            def _():
                lax.fori_loop(0, E, one, 0)

        def gate_rows(t):
            return pl.ds(pl.multiple_of(t * GROWS, GROWS), GROWS)

        def enter(t):
            for k in range(2):
                cols = slice(k * (R // 2), (k + 1) * (R // 2))
                flipped = inbox[t, cols].T
                hi, lo = split(flipped)
                u_next[:D, cols] = hi
                u_next[D : 2 * D, cols] = hi
                u_next[2 * D :, cols] = lo
                acc[:, cols] = flipped
                yield
            logits = mm(wide(wg[gate_rows(t)]), u_next[...])
            cs_next[...] = logits
            yield
            u_n[t] = tall(inbox[t])
            yield
            _, r, mix, _, _ = gate_state(logits, 1)
            yield
            for j in range(E):
                gt_next[j] = over_selectors(mix * r[j], 1, jnp.add)
                yield

        def turn():
            u_t[...] = u_next[...]
            gt[...] = gt_next[...]
            cs[GROWS : 2 * GROWS] = cs[:GROWS]
            cs[:GROWS] = cs_next[...]

        def leave(t, at):
            out = []
            yield from gate_backward(cs[at : at + GROWS], lambda j: dgt[j, 0:1], 1, out)
            outbox[t] = acc_b[...] + t_dot(wg[gate_rows(t)], out[0])
            yield
            dg[gate_rows(t)] = mm(wide(out[0]), u_n[t])
            yield

        def all_of(pieces):
            for _ in pieces:
                pass

        cs[...] = jnp.zeros_like(cs)
        dgt[...] = jnp.zeros_like(dgt)
        acc_b[...] = jnp.zeros_like(acc_b)
        copy(outbox.at[0], inbox.at[0], K_UP, across).wait_recv()
        all_of(enter(0))
        turn()

        def task(t, carry):
            @pl.when(t > 0)
            def _():
                keep(0, 0).wait()

            def first(j, par):
                bb[par] = mm(pair(wt[j]), u_t[...])

            def activate(j, par, part_no):
                for tile in halves(H)[part_no]:
                    value, slope = gelu_pair(bb[par, tile])
                    a1[shifted(tile, j)] = value
                    a2[shifted(tile, j)] = slope
                    put(gbuf, (j, tile), value * gt[j])

            def finish(j, par):
                acc[...] += mm(pair(wt[E + j]), stack(gbuf[j]))

            before = (t + TASKS - 1) % TASKS
            weave(E, first, activate, finish, leave(before, GROWS))
            keep_start(0, t)

            @pl.when(t > 0)
            def _():
                copy(outbox.at[before], inbox.at[before], K_DOWN + before, across).start()

            second = acc[...]
            held[...] = second
            tower = ti[t]
            g, slope = gelu_pair(mm(wide(tower.T), tall(second)))
            info = sm[t]
            out_col = info[:, :TOWER].T[:, 2:3]
            here = sm[t, :, mine]
            logit = jnp.sum(g * out_col, axis=0, keepdims=True) + here[3:4]
            prob = jax.nn.sigmoid(logit)
            dlogit = here[1:2] * (prob - here[0:1])
            m = dlogit * out_col * slope
            dy = mm(wide(tower), tall(m))
            s_t[...] = tall(dy)
            acc_b[...] = dy
            dy_kept[...] = dy
            tm[:TOWER] = m
            tm[TOWER:] = g * dlogit
            tp[t, TOWER : TOWER + 1] = prob
            tp[t, TOWER + 2 : TOWER + 3] = dlogit
            tp[t, TOWER + 3 :] = jnp.zeros((5, R), F32)

            @pl.when(t > 0)
            def _():
                keep(1, 0).wait()

            @pl.when(t == TASKS - 1)
            def _():
                for i in range(AHEAD):
                    fetch_start(i)

            after = jnp.minimum(t + 1, TASKS - 1)

            @pl.when(t < TASKS - 1)
            def _():
                copy(outbox.at[after], inbox.at[after], K_UP + after, across).wait_recv()

            def back(j, par):
                bb[par] = mm(pair(w_out[j]), s_t[...])

            def pull(j, par, part_no):
                total = jnp.zeros((8, R), F32)
                for tile in halves(H)[part_no]:
                    grad = bb[par, tile]
                    total = total + rows8(grad * a1[shifted(tile, j)])
                    put(kbuf, (j, tile), grad * a2[shifted(tile, j)] * gt[j])
                total = jnp.sum(total, axis=0, keepdims=True)
                if part_no == 0:
                    dgt[j, 0:1] = total
                else:
                    dgt[j, 0:1] += total

            def spread(j, par):
                acc_b[...] += mm(pair(w_in[j]), stack(kbuf[j]))

            def beside():
                s_n[t] = tall(dy_kept[...].T)
                yield
                yield from enter(after)
                flipped = tall(held[...].T)
                yield
                tp[t, :TOWER] = mm(wide(tm[:TOWER]), flipped)
                yield
                out_grad = jnp.sum(tm[TOWER:], axis=1, keepdims=True)
                out_row = jnp.broadcast_to(out_grad, (TOWER, TOWER)).T[0:1]
                tp[t, TOWER + 1 : TOWER + 2] = jnp.concatenate([out_row, jnp.zeros_like(out_row)], axis=1)
                yield

            weave(E, back, pull, spread, beside())
            keep_start(1, t)
            turn()

            @pl.when(t != s)
            def _():
                copy(tp.at[t], tw.at[c], K_TW + c, t, K_TW + t).start()

            @pl.when(t == s)
            def _():
                tw[c] = tp[t]

            return carry

        lax.fori_loop(0, TASKS, task, 0)
        last_task = TASKS - 1
        all_of(leave(last_task, GROWS))
        copy(outbox.at[last_task], inbox.at[last_task], K_DOWN + last_task, across).start()
        greet_ring()

    @pl.when(x == 1)
    def _():
        def one(i, carry):
            fetch(i).wait()

            @pl.when(i < E - AHEAD)
            def _():
                fetch_start(i + AHEAD)

            j = turn_of(i)
            slot_at = (i % (AHEAD + 1)) * 8
            for k, (grad, right, here) in enumerate(((d_out, s_n, gbuf), (d_in, u_n, kbuf))):
                left = [pair(wt[slot_at + k * SPILL + t]) for t in range(SPILL)] + [pair(here[j])]
                grad[expert(j)] = mm(jnp.concatenate(left, axis=1), right[...].reshape(3 * TASKS * R, D))

            @pl.when(i % 2 == 0)
            def _():
                for move in give(near(i // 2)):
                    move.start()

            @pl.when(i == 3)
            def _():
                merge(0, 0)
                ring_start()

            @pl.when((i % 2 == 1) & (i > 3))
            def _():
                merge((i - 3) // 2, 0)

            if n == HALF:

                @pl.when((i % 4 == 3) & (i > 3))
                def _():
                    reduce_step((i - 3) // 4, 0)

            return carry

        lax.fori_loop(0, E, one, 0)
        merge(HALF - 1, 0)
        if n != HALF:
            lax.fori_loop(1, 4, reduce_step, 0)

    @pl.when(x == 0)
    def _():
        def arrive(t, carry):
            copy(outbox.at[t], inbox.at[t], K_DOWN + t, across).wait_recv()
            acc[...] += inbox[t]

            def one(j, inner):
                gate = gt0[j, pl.ds(t, 1)]
                total = jnp.zeros((8, R), F32)
                for tile in rows_of(D):
                    dy = inbox[t, tile]
                    rows = pl.ds(pl.multiple_of(j * D + tile.start, TILE), TILE)
                    total = total + rows8(d_in[rows] * dy)
                    d_out[rows] += gate * dy
                dgt[j, pl.ds(t, 1)] = jnp.sum(total, axis=0, keepdims=True)
                return inner

            lax.fori_loop(0, E, one, 0)
            return carry

        lax.fori_loop(0, TASKS - 1, arrive, 0)
        last = TASKS - 1
        copy(outbox.at[last], inbox.at[last], K_DOWN + last, across).wait_recv()
        acc[...] += inbox[last]

        def one(i, inner):
            j = turn_of(i)
            gate = gt0[j, last : last + 1]
            total = jnp.zeros((8, R), F32)
            for tile in rows_of(D):
                dy = inbox[last, tile]
                rows = pl.ds(pl.multiple_of(j * D + tile.start, TILE), TILE)
                total = total + rows8(d_in[rows] * dy)
                put(kbuf.at[j], (tile,), d_out[rows] + gate * dy)
            dgt[j, last : last + 1] = jnp.sum(total, axis=0, keepdims=True)
            return inner

        def part_of(first, stop):
            lax.fori_loop(2 * first, 2 * stop, one, 0)

            def products(i, par):
                j = turn_of(2 * first + i)
                mixed = kbuf[j]
                bb[par] = mm(pair(w_out[j]), stack(mixed))
                right = jnp.concatenate([mixed[:, :R], mixed[:, :R], mixed[:, R:]], axis=1)
                d_out[expert(j)] = lax.dot_general(
                    pair(gbuf[j]), right, (((1,), (1,)), ((), ())), preferred_element_type=F32
                )

            def pull(i, par, part_no):
                j = turn_of(2 * first + i)
                for tile in halves(H)[part_no]:
                    kept_rows = pl.ds(pl.multiple_of(j * H + tile.start, TILE), TILE)
                    put(kp, (par, tile), bb[par, tile] * a2[kept_rows])

            def spread(i, par):
                j = turn_of(2 * first + i)
                acc[...] += mm(pair(w_in[j]), stack(kp[par]))
                d_in[expert(j)] = mm(pair(kp[par]), u_n[0])

            weave(2 * (stop - first), products, pull, spread)
            for k in range(first, stop):
                for move in give(near(k)):
                    move.start()

        part_of(0, 1)
        part_of(1, 4)
        merge(0, 0)
        ring_start()
        part_of(4, HALF)
        lax.fori_loop(1, HALF, merge, 0)
        lax.fori_loop(1, 2, reduce_step, 0)

    gates_own = pl.ds(pl.multiple_of(c * 2 * GROWS, 2 * GROWS), 2 * GROWS)
    gates_away = pl.ds(pl.multiple_of((1 - c) * 2 * GROWS, 2 * GROWS), 2 * GROWS)
    gain_row[...] = jnp.zeros_like(gain_row)

    @pl.when(x == 0)
    def _():
        out = []
        for _ in gate_backward(cs[...], lambda j: dgt[j, :TASKS], TASKS, out):
            pass
        dc = out[0]
        dpool = (acc[...] + t_dot(wg[:FROWS], dc)).T
        pre_rows = pre[...]
        rho = lax.rsqrt(jnp.mean(pre_rows * pre_rows, axis=1, keepdims=True) + NORM_EPS)
        scaled = dpool * gain_ref[...]
        dots = jnp.mean(scaled * pre_rows, axis=1, keepdims=True)
        dp[mine] = rho * scaled - pre_rows * (rho * rho * rho * dots)
        for k, sec in enumerate((mate, across, diag)):
            copy(dp.at[mine], dp.at[mine], K_DP + c, sec, K_DP + k).start()
        gain_row[0:1] = jnp.sum(dpool * pre_rows * rho, axis=0, keepdims=True)
        grad = mm(wide(dc), u_n[0])
        dg[: FROWS // 2] = grad[: FROWS // 2]
        dg[2 * GROWS : 2 * GROWS + FROWS // 2] = grad[FROWS // 2 :]

    gates_move = copy(dg.at[gates_away], gb, K_DG, mate)
    gates_move.start()

    @pl.when(x == 0)
    def _():
        lax.fori_loop(2, 4, reduce_step, 0)

    for half_no in range(2):

        @pl.when(s != half_no)
        def _():
            rows = pl.ds(half_no * R, R)
            copy(dp.at[rows], dp.at[rows], K_DP + half_no, half_no).wait_recv()

    for k in range(2):

        @pl.when(s != 2 + k)
        def _():
            copy(tp.at[0], tw.at[k], K_TW + k, s).wait_recv()

    gates_move.wait_recv()
    sb[:TOWER] = tw[0, :TOWER] + tw[1, :TOWER]
    sb[GATE_AT:MISC_AT] = dg[gates_own] + gb[...]
    sb[MISC_AT : MISC_AT + 1] = gain_row[0:1]
    sb[MISC_AT + 1 : MISC_AT + 3] = tw[0, TOWER + 1 : TOWER + 3] + tw[1, TOWER + 1 : TOWER + 3]
    for f in range(2):
        sb[MISC_AT + 3 + f : MISC_AT + 4 + f] = jnp.sum(xf[f] * dp[...], axis=0, keepdims=True)
    sb[MISC_AT + 5 : MISC_AT + 6] = smo[1:2, :R] + smo[1:2, R:]
    sb[MISC_AT + 6 :] = jnp.zeros((sb.shape[0] - MISC_AT - 6, D), F32)

    def block(q):
        return pl.ds(pl.multiple_of(q * small_rows, 8), small_rows)

    def scatter(i):
        to = (me + i) % n
        return pltpu.make_async_remote_copy(
            src_ref=sb.at[block(to)],
            dst_ref=sr.at[me],
            send_sem=sr_send.at[i],
            recv_sem=sr_recv.at[me],
            device_id={"dp": to},
            device_id_type=MESH,
        )

    def scattered(i):
        by = (me + i) % n
        return pltpu.make_async_remote_copy(
            src_ref=sb.at[block(me)],
            dst_ref=sr.at[by],
            send_sem=sr_send.at[i],
            recv_sem=sr_recv.at[by],
            device_id={"dp": by},
            device_id_type=MESH,
        )

    def spread_sum(i):
        return pltpu.make_async_remote_copy(
            src_ref=so,
            dst_ref=sa.at[block(me)],
            send_sem=sa_send.at[i],
            recv_sem=sa_recv.at[me],
            device_id={"dp": (me + i) % n},
            device_id_type=MESH,
        )

    def gathered(i):
        by = (me + i) % n
        return pltpu.make_async_remote_copy(
            src_ref=so,
            dst_ref=sa.at[block(by)],
            send_sem=sa_send.at[i],
            recv_sem=sa_recv.at[by],
            device_id={"dp": by},
            device_id_type=MESH,
        )

    def each(act):
        def one(i, carry):
            act(i)
            return carry

        lax.fori_loop(1, n, one, 0)

    each(lambda i: scatter(i).start())
    lax.fori_loop(4, 5, reduce_step, 0)
    so[...] = sb[block(me)]

    def take(i):
        scattered(i).wait_recv()
        so[...] += sr[(me + i) % n]

    each(take)
    sa[block(me)] = so[...]
    each(lambda i: spread_sum(i).start())
    lax.fori_loop(5, 6, reduce_step, 0)
    each(lambda i: gathered(i).wait_recv())
    piece = sa.at[pl.ds(GATE_AT, KEPT)]
    for k, sec in enumerate((mate, across, diag)):
        copy(piece, sg.at[s], K_GO + s, sec, K_GO + k).start()
    sg[s] = sa[GATE_AT:SMALL]
    lax.fori_loop(6, n - 1, reduce_step, 0)
    for sec in (mate, across, diag):
        copy(piece, sg.at[sec], K_GO + sec, sec).wait_recv()
    misc = KEPT - 8
    count = sum(sg[q, misc + 5 : misc + 6] for q in range(TASKS))
    scale = float(2 * R * n) / jnp.sum(count, axis=1, keepdims=True)

    last = n - 2
    for d, k in lanes:
        q = holds(d, n - 1)
        rs(d, k, last, a1.at[slot(d, k, last)]).wait_recv()
        a1[slot(d, k, last)] = (a1[slot(d, k, last)] + rd[d, at(k, q)]) * scale
        ag(d, k, 0, a1.at[slot(d, k, last)], q).start()
        store(d, k, q, a1.at[slot(d, k, last)], 0).start()

    for f in range(2):
        xf[f] = dp[...] * (scale * fw_ref[0, f])
        pltpu.make_async_copy(xf.at[f], o_ig.at[:, f], local.at[2 + f]).start()
    for k in range(2):
        o_pred[:, k * R : (k + 1) * R] = tw[k, TOWER : TOWER + 1]
    for f in range(2):
        o_fw[0, f] = jnp.sum(sa[MISC_AT + 3 + f : MISC_AT + 4 + f] * scale)
    o_bias[0, 0] = jnp.sum(sa[MISC_AT + 2 : MISC_AT + 3] * scale)
    o_gain[...] = (sg[0, misc : misc + 1] + sg[1, misc : misc + 1]) * scale
    o_tout[...] = sa[MISC_AT + 1 : MISC_AT + 2, :TOWER] * scale
    o_tin[...] = (sa[:TOWER] * scale).T

    def order(t, carry):
        for sel in range(SEL):
            for e in range(BITS + 1):
                row = t * (SEL * (BITS + 1)) + sel * (BITS + 1) + e
                at0 = (e * SEL + sel) * TASKS
                cut = FROWS // 2
                o_gate[0, pl.ds(row, 1)] = sg[at0 // cut, pl.ds(at0 % cut + t, 1)] * scale
                o_gate[1, pl.ds(row, 1)] = sg[2 + t // 2, pl.ds((t % 2) * GROWS + e * SEL + sel, 1)] * scale
        return carry

    lax.fori_loop(0, TASKS, order, 0)

    def gather_step(step, carry):
        for d, k in lanes:
            q = holds(d, step - 1)
            ag(d, k, step - 1, landed(d, k, q), q).wait_recv()
            ag(d, k, step, landed(d, k, q), q).start()
            store(d, k, q, landed(d, k, q), step).start()
        return carry

    lax.fori_loop(1, n - 1, gather_step, 0)
    for d, k in lanes:
        q = holds(d, n - 2)
        ag(d, k, last, landed(d, k, q), q).wait_recv()
        store(d, k, q, landed(d, k, q), n - 1).start()

    def stored(step, carry):
        for d, k in lanes:
            store(d, k, 0, landed(d, k, 0), step).wait()
        return carry

    lax.fori_loop(0, n, stored, 0)

    def sent(step, carry):
        for d, k in lanes:
            rs(d, k, step, a1.at[slot(d, k, step)]).wait_send()
            ag(d, k, step, a1.at[slot(d, k, step)], 0).wait_send()
        return carry

    lax.fori_loop(0, n - 1, sent, 0)
    each(lambda i: scatter(i).wait_send())
    each(lambda i: spread_sum(i).wait_send())
    to_mate.wait_send()
    gates_move.wait_send()
    for e in range(HALF):
        for move in give(e):
            move.wait_send()
    for k in range(2):

        @pl.when(s != 2 + k)
        def _():
            copy(smo, sm.at[s], K_SM + s, 2 + k, K_SM + k).wait_send()
            copy(tin_ref, ti.at[s], K_TI + s, 2 + k, K_TI + k).wait_send()

    @pl.when(x == 0)
    def _():
        for t in range(TASKS):
            copy(outbox.at[t], inbox.at[t], K_UP + t, across).wait_send()
        for k, sec in enumerate((mate, across, diag)):
            copy(dp.at[mine], dp.at[mine], K_DP + c, sec, K_DP + k).wait_send()

    @pl.when(x == 1)
    def _():
        copy(pre2, pre1, K_P + 1, across).wait_send()
        for t in range(TASKS):
            copy(outbox.at[t], inbox.at[t], K_DOWN + t, across).wait_send()

            @pl.when(t != s)
            def _():
                copy(tp.at[t], tw.at[c], K_TW + c, t, K_TW + t).wait_send()

    for k, sec in enumerate((mate, across, diag)):
        copy(piece, sg.at[s], K_GO + s, sec, K_GO + k).wait_send()
    for f in range(2):
        pltpu.make_async_copy(xf.at[f], o_ig.at[:, f], local.at[2 + f]).wait()


def hand_over(count, *refs):
    held = refs[2 * count : 3 * count]
    sems = refs[-1]
    reads = [pltpu.make_async_copy(refs[k], held[k], sems.at[0, k]) for k in range(count)]
    writes = [pltpu.make_async_copy(held[k], refs[count + k], sems.at[1, k]) for k in range(count)]
    for move in reads:
        move.start()
    for read, write in zip(reads, writes):
        read.wait()
        write.start()
    for move in writes:
        move.wait()


def body(
    field_inputs,
    field_weight,
    norm_gain,
    gate_weight,
    expert_in,
    expert_out,
    tower_in,
    tower_out,
    tower_bias,
    labels,
    source_ids,
    task_table,
):
    n = lax.axis_size("dp")
    rows = field_inputs.shape[0]
    half = rows // 2
    subs = 2
    small_rows = -(-SMALL // (8 * n)) * 8
    used = TASKS * SEL * (BITS + 1)

    vmem = pl.BlockSpec(memory_space=pltpu.VMEM)
    smem = pl.BlockSpec(memory_space=pltpu.SMEM)
    hbm = pl.BlockSpec(memory_space=pl.ANY)

    def bf(*shape):
        return pltpu.VMEM(shape, BF16)

    def f32(*shape):
        return pltpu.VMEM(shape, F32)

    def out(*shape):
        return jax.ShapeDtypeStruct(shape, F32)

    dma = pltpu.SemaphoreType.DMA
    *sums, _ = pl.pallas_call(
        partial(kernel, n, subs, small_rows),
        out_shape=(
            out(1, rows),
            out(rows, 2, D),
            out(1, 2),
            out(1, D),
            out(2, used, D),
            out(HALF * H, D),
            out(HALF * H, D),
            out(D, TOWER),
            out(1, TOWER),
            out(1, 1),
            jax.ShapeDtypeStruct((E, 2 * SPILL, H, 2 * half), BF16),
        ),
        in_specs=[hbm, smem, vmem, vmem, hbm, hbm, vmem, vmem, smem, vmem, vmem, smem],
        out_specs=(vmem, hbm, smem, vmem, vmem, hbm, hbm, vmem, vmem, smem, hbm),
        scratch_shapes=[
            bf(2 * E, H, 2 * D),
            bf(E, D, 2 * H),
            bf(E, H, 2 * D),
            f32(E * H, half),
            f32(E * H, half),
            f32(E * H, D),
            f32(E * H, D),
            bf(E, H, 2 * half),
            bf(E, H, 2 * half),
            bf(2, H, 2 * half),
            f32(2, HALF * H, D),
            f32(2, rows, D),
            f32(rows, D),
            f32(half, D),
            f32(half, D),
            f32(half, D),
            f32(half, D),
            f32(TASKS, D, half),
            f32(TASKS, D, half),
            bf(3 * D, half),
            bf(TASKS, 3 * half, D),
            bf(3 * D, half),
            bf(TASKS, 3 * half, D),
            f32(2, H, half),
            f32(D, half),
            f32(TASKS * GROWS, D),
            f32(E, 1, half),
            f32(E, TASKS, half),
            f32(FROWS, half),
            f32(E, TASKS, half),
            f32(TASKS * GROWS, D),
            f32(2 * GROWS, D),
            f32(TASKS, 8, rows),
            f32(8, rows),
            f32(TASKS, D, TOWER),
            f32(TASKS, TOWER + 8, D),
            f32(2, TOWER + 8, D),
            f32(rows, D),
            f32(8, D),
            f32(half, E * TASKS),
            bf(3 * D, half),
            f32(E, 1, half),
            f32(GROWS, half),
            f32(D, half),
            f32(D, half),
            f32(D, half),
            f32(2 * TOWER, half),
            f32(n * small_rows, D),
            f32(n, small_rows, D),
            f32(small_rows, D),
            f32(n * small_rows, D),
            f32(TASKS, KEPT, D),
            dma((K_COUNT,)),
            dma((K_COUNT,)),
            dma((6,)),
            dma((AHEAD + 1,)),
            pltpu.SemaphoreType.REGULAR,
            dma((2, subs, n - 1)),
            dma((2, subs, n - 1)),
            dma((2, subs, n - 1)),
            dma((2, subs, n - 1)),
            dma((2, subs, n)),
            dma((n,)),
            dma((n,)),
            dma((n,)),
            dma((n,)),
        ],
        compiler_params=pltpu.CompilerParams(
            collective_id=0, has_side_effects=True, vmem_limit_bytes=64 * 1024 * 1024 - 65536
        ),
    )(
        field_inputs,
        field_weight.reshape(1, 2),
        norm_gain.reshape(1, D),
        gate_weight.swapaxes(1, 2),
        expert_in.reshape(HALF * H, D),
        expert_out.reshape(HALF * H, D),
        tower_in.reshape(D, TOWER),
        tower_out,
        tower_bias.reshape(1, 1),
        labels.reshape(1, rows),
        source_ids.reshape(1, rows),
        task_table.reshape(1, SOURCES),
    )
    pred, ig, fw, gain, gate, d_in, d_out, tin, tout, bias = pl.pallas_call(
        partial(hand_over, len(sums)),
        out_shape=tuple(jax.ShapeDtypeStruct(v.shape, v.dtype) for v in sums),
        in_specs=[hbm] * len(sums),
        out_specs=(hbm,) * len(sums),
        scratch_shapes=[pltpu.VMEM(v.shape, v.dtype) for v in sums] + [dma((2, len(sums)))],
        compiler_params=pltpu.CompilerParams(vmem_limit_bytes=64 * 1024 * 1024 - 65536),
    )(*sums)
    return (
        pred.reshape(rows, 1),
        ig,
        fw.reshape(2),
        gain.reshape(D),
        gate.swapaxes(1, 2),
        d_in.reshape(HALF, D, H),
        d_out.reshape(HALF, H, D),
        tin.reshape(1, D, TOWER),
        tout,
        bias.reshape(1),
    )


def solution(mesh):
    in_specs = (
        P("dp", "section", None),
        P("section"),
        P(),
        P(),
        P("section", None, None),
        P("section", None, None),
        P("section", None, None),
        P("section", None),
        P("section"),
        P("dp", "section"),
        P("dp"),
        P(None, "section"),
    )
    out_specs = (
        P("dp", "section"),
        P("dp", "section", None),
        P("section"),
        P(),
        P(),
        P("section", None, None),
        P("section", None, None),
        P("section", None, None),
        P("section", None),
        P("section"),
    )
    return jax.shard_map(body, mesh=mesh, in_specs=in_specs, out_specs=out_specs, check_vma=False)
```

profile of v0, /device:TPU:0, one launch (start us, length us, event | category | flops | bytes accessed | tf_op | source)
XLA Modules:
  0.0 185.1 jit_solution(10084154495594569552)
XLA Ops:
  1.3 178.1 %shard_map.195 = (f32[1,512]{1,0:T(1,128)}, f32[512,2,256]{2,1,0:T(2,128)}, f32[1,2]{1,0:T(1,128)}, f32[1,256]{1,0:T(1,128)}, f32[2,80,256]{2,1,0:T(8,128)}, /*i...) custom-call(f32[512,2,256]{2,1,0:T(2,128)} %x_ref.1, ...), custom_call_target="tpu_custom_call" | custom-call | tf_op jit(solution)/shard_map/pallas_call | solution.py:1140
  179.4 5.4 %shard_map.196 = (f32[1,512]{1,0:T(1,128)}, f32[512,2,256]{2,1,0:T(2,128)}, f32[1,2]{1,0:T(1,128)}, f32[1,256]{1,0:T(1,128)}, f32[2,80,256]{2,1,0:T(8,128)}, /*i...) custom-call(f32[1,512]{1,0:T(1,128)} %get-tuple-element.30.refs_0_, ...), custom_call_target="tpu_custom_call" | custom-call | tf_op jit(solution)/shard_map/pallas_call | solution.py:1242
where the time goes:
time: 185 us
  Pallas kernels  184 us (99%)
    pallas_call x1, Pallas kernels, body(): pl.pallas_call(partial(kernel, n, subs, small_rows), out_shape=(out(1, ro...  178 us
    pallas_call x1, Pallas kernels, body(): pl.pallas_call(partial(hand_over, len(sums)), out_shape=tuple((jax.ShapeD...  5.44 us

commit v1 on v0

--- a/solution.py
+++ b/solution.py
@@ -206,6 +206,7 @@
     o_tin,
     o_tout,
     o_bias,
+    o_scale,
     kept,
     wt,
     w_in,
@@ -331,12 +332,12 @@
     part[...] = xf[0] * fw_ref[0, 0] + xf[1] * fw_ref[0, 1]
     to_mate = copy(part.at[theirs], pre0, K_P, mate)
     to_mate.start()
-    swap_in = copy(d_in.at[own], d_in.at[own], K_W, mate)
-    swap_out = copy(d_out.at[own], d_out.at[own], K_W + 1, mate)
+    swap_in = copy(win_ref, d_in.at[own], K_W, mate)
+    swap_out = copy(wout_ref, d_out.at[own], K_W + 1, mate)
+    swap_in.start()
+    swap_out.start()
     own_in.wait()
-    swap_in.start()
     own_out.wait()
-    swap_out.start()
 
     ids = ids_ref[...]
     mask = jnp.zeros(ids.shape, F32)
@@ -398,9 +399,11 @@
         return carry
 
     lax.fori_loop(c * HALF, c * HALF + HALF, keep_plain, 0)
-    swap_in.wait()
-    swap_out.wait()
-    lax.fori_loop((1 - c) * HALF, (1 - c) * HALF + HALF, keep_plain, 0)
+
+    def keep_mates():
+        swap_in.wait()
+        swap_out.wait()
+        lax.fori_loop((1 - c) * HALF, (1 - c) * HALF + HALF, keep_plain, 0)
 
     def rows_of(size):
         return [slice(a, a + TILE) for a in range(0, size, TILE)]
@@ -517,21 +520,29 @@
         for j, g in enumerate(gates):
             gt0[j] = g
 
-        def first(j, par):
-            left = jnp.concatenate([u_n[0, :R], u_n[0, 2 * R :], u_n[0, :R]], axis=1)
-            bb[par] = mm(left, stack(w_in[j]))
-
-        def activate(j, par, part_no):
-            for tile in halves(R)[part_no]:
-                value, slope = gelu_pair(bb[par, tile])
-                a1[shifted(tile, j)] = value
-                a2[shifted(tile, j)] = slope
-                put(gbuf, (j, tile), value)
-
-        def finish(j, par):
-            d_in[expert(j)] = mm(pair(gbuf[j]), stack(w_out[j]))
-
-        weave(E, first, activate, finish)
+        def rows_at(j, tile):
+            return pl.ds(pl.multiple_of(j * H + tile.start, TILE), TILE)
+
+        def forward(base):
+            def first(i, par):
+                left = jnp.concatenate([u_n[0, :R], u_n[0, 2 * R :], u_n[0, :R]], axis=1)
+                bb[par] = mm(left, stack(w_in[base + i]))
+
+            def activate(i, par, part_no):
+                for tile in halves(R)[part_no]:
+                    value, slope = gelu_pair(bb[par, tile])
+                    a1[rows_at(base + i, tile)] = value
+                    a2[rows_at(base + i, tile)] = slope
+                    put(gbuf, (base + i, tile), value)
+
+            def finish(i, par):
+                d_in[expert(base + i)] = mm(pair(gbuf[base + i]), stack(w_out[base + i]))
+
+            weave(HALF, first, activate, finish)
+
+        forward(c * HALF)
+        keep_mates()
+        forward((1 - c) * HALF)
         columns[...] = jnp.concatenate(gates, axis=0).T
 
         for t in range(TASKS):
@@ -564,6 +575,7 @@
 
     @pl.when(x == 1)
     def _():
+        keep_mates()
         lax.fori_loop(0, E, keep_flipped, 0)
         for q in range(TASKS):
 
@@ -854,12 +866,17 @@
                     move.start()
 
         part_of(0, 1)
-        part_of(1, 4)
+        part_of(1, 2)
         merge(0, 0)
         ring_start()
-        part_of(4, HALF)
-        lax.fori_loop(1, HALF, merge, 0)
-        lax.fori_loop(1, 2, reduce_step, 0)
+        for k in range(2, HALF, 2):
+            part_of(k, k + 2)
+            lax.fori_loop(k - 1, k + 1, merge, 0)
+            if n == HALF:
+                reduce_step(k // 2, 0)
+        merge(HALF - 1, 0)
+        if n != HALF:
+            lax.fori_loop(1, HALF // 2, reduce_step, 0)
 
     gates_own = pl.ds(pl.multiple_of(c * 2 * GROWS, 2 * GROWS), 2 * GROWS)
     gates_away = pl.ds(pl.multiple_of((1 - c) * 2 * GROWS, 2 * GROWS), 2 * GROWS)
@@ -887,9 +904,7 @@
     gates_move = copy(dg.at[gates_away], gb, K_DG, mate)
     gates_move.start()
 
-    @pl.when(x == 0)
-    def _():
-        lax.fori_loop(2, 4, reduce_step, 0)
+    lax.fori_loop(4, 6, reduce_step, 0)
 
     for half_no in range(2):
 
@@ -968,7 +983,23 @@
         lax.fori_loop(1, n, one, 0)
 
     each(lambda i: scatter(i).start())
-    lax.fori_loop(4, 5, reduce_step, 0)
+    lax.fori_loop(6, n - 1, reduce_step, 0)
+    last = n - 2
+    for d, k in lanes:
+        q = holds(d, n - 1)
+        rs(d, k, last, a1.at[slot(d, k, last)]).wait_recv()
+        a1[slot(d, k, last)] += rd[d, at(k, q)]
+        ag(d, k, 0, a1.at[slot(d, k, last)], q).start()
+        store(d, k, q, a1.at[slot(d, k, last)], 0).start()
+
+    def gather_step(step, carry):
+        for d, k in lanes:
+            q = holds(d, step - 1)
+            ag(d, k, step - 1, landed(d, k, q), q).wait_recv()
+            ag(d, k, step, landed(d, k, q), q).start()
+            store(d, k, q, landed(d, k, q), step).start()
+        return carry
+
     so[...] = sb[block(me)]
 
     def take(i):
@@ -978,26 +1009,20 @@
     each(take)
     sa[block(me)] = so[...]
     each(lambda i: spread_sum(i).start())
-    lax.fori_loop(5, 6, reduce_step, 0)
+    lax.fori_loop(1, 3, gather_step, 0)
     each(lambda i: gathered(i).wait_recv())
     piece = sa.at[pl.ds(GATE_AT, KEPT)]
     for k, sec in enumerate((mate, across, diag)):
         copy(piece, sg.at[s], K_GO + s, sec, K_GO + k).start()
     sg[s] = sa[GATE_AT:SMALL]
-    lax.fori_loop(6, n - 1, reduce_step, 0)
+    lax.fori_loop(3, 4, gather_step, 0)
     for sec in (mate, across, diag):
         copy(piece, sg.at[sec], K_GO + sec, sec).wait_recv()
     misc = KEPT - 8
     count = sum(sg[q, misc + 5 : misc + 6] for q in range(TASKS))
     scale = float(2 * R * n) / jnp.sum(count, axis=1, keepdims=True)
 
-    last = n - 2
-    for d, k in lanes:
-        q = holds(d, n - 1)
-        rs(d, k, last, a1.at[slot(d, k, last)]).wait_recv()
-        a1[slot(d, k, last)] = (a1[slot(d, k, last)] + rd[d, at(k, q)]) * scale
-        ag(d, k, 0, a1.at[slot(d, k, last)], q).start()
-        store(d, k, q, a1.at[slot(d, k, last)], 0).start()
+    o_scale[...] = jnp.broadcast_to(scale, o_scale.shape)
 
     for f in range(2):
         xf[f] = dp[...] * (scale * fw_ref[0, f])
@@ -1023,15 +1048,7 @@
 
     lax.fori_loop(0, TASKS, order, 0)
 
-    def gather_step(step, carry):
-        for d, k in lanes:
-            q = holds(d, step - 1)
-            ag(d, k, step - 1, landed(d, k, q), q).wait_recv()
-            ag(d, k, step, landed(d, k, q), q).start()
-            store(d, k, q, landed(d, k, q), step).start()
-        return carry
-
-    lax.fori_loop(1, n - 1, gather_step, 0)
+    lax.fori_loop(4, n - 1, gather_step, 0)
     for d, k in lanes:
         q = holds(d, n - 2)
         ag(d, k, last, landed(d, k, q), q).wait_recv()
@@ -1088,16 +1105,26 @@
         pltpu.make_async_copy(xf.at[f], o_ig.at[:, f], local.at[2 + f]).wait()
 
 
-def hand_over(count, *refs):
+def hand_over(count, scaled, scale_ref, *refs):
     held = refs[2 * count : 3 * count]
     sems = refs[-1]
     reads = [pltpu.make_async_copy(refs[k], held[k], sems.at[0, k]) for k in range(count)]
     writes = [pltpu.make_async_copy(held[k], refs[count + k], sems.at[1, k]) for k in range(count)]
-    for move in reads:
-        move.start()
-    for read, write in zip(reads, writes):
-        read.wait()
-        write.start()
+    order = list(scaled) + [k for k in range(count) if k not in scaled]
+    for k in order:
+        reads[k].start()
+    scale = scale_ref[0:1, 0:1]
+    for k in order:
+        reads[k].wait()
+        if k in scaled:
+
+            def one(i, carry):
+                rows = pl.ds(pl.multiple_of(i * H, H), H)
+                held[k][rows] = held[k][rows] * scale
+                return carry
+
+            lax.fori_loop(0, held[k].shape[0] // H, one, 0)
+        writes[k].start()
     for move in writes:
         move.wait()
 
@@ -1137,7 +1164,7 @@
         return jax.ShapeDtypeStruct(shape, F32)
 
     dma = pltpu.SemaphoreType.DMA
-    *sums, _ = pl.pallas_call(
+    *sums, scale, _ = pl.pallas_call(
         partial(kernel, n, subs, small_rows),
         out_shape=(
             out(1, rows),
@@ -1150,10 +1177,11 @@
             out(D, TOWER),
             out(1, TOWER),
             out(1, 1),
+            out(1, TOWER),
             jax.ShapeDtypeStruct((E, 2 * SPILL, H, 2 * half), BF16),
         ),
         in_specs=[hbm, smem, vmem, vmem, hbm, hbm, vmem, vmem, smem, vmem, vmem, smem],
-        out_specs=(vmem, hbm, smem, vmem, vmem, hbm, hbm, vmem, vmem, smem, hbm),
+        out_specs=(vmem, hbm, smem, vmem, vmem, hbm, hbm, vmem, vmem, smem, vmem, hbm),
         scratch_shapes=[
             bf(2 * E, H, 2 * D),
             bf(E, D, 2 * H),
@@ -1240,13 +1268,13 @@
         task_table.reshape(1, SOURCES),
     )
     pred, ig, fw, gain, gate, d_in, d_out, tin, tout, bias = pl.pallas_call(
-        partial(hand_over, len(sums)),
+        partial(hand_over, len(sums), (5, 6)),
         out_shape=tuple(jax.ShapeDtypeStruct(v.shape, v.dtype) for v in sums),
-        in_specs=[hbm] * len(sums),
+        in_specs=[vmem] + [hbm] * len(sums),
         out_specs=(hbm,) * len(sums),
         scratch_shapes=[pltpu.VMEM(v.shape, v.dtype) for v in sums] + [dma((2, len(sums)))],
         compiler_params=pltpu.CompilerParams(vmem_limit_bytes=64 * 1024 * 1024 - 65536),
-    )(*sums)
+    )(scale, *sums)
     return (
         pred.reshape(rows, 1),
         ig,

time: 185 us -> 186 us (level)
  no operation moved by 1% of the time
where the time goes in v1:
time: 186 us; the launch traced here: 185 us
  Pallas kernels  184 us (99%)
    pallas_call x1, Pallas kernels, body(): pl.pallas_call(partial(kernel, n, subs, small_rows), out_shape=(out(1, ro...  178 us
    pallas_call x1, Pallas kernels, body(): pl.pallas_call(partial(hand_over, len(sums), (5, 6)), out_shape=tuple((ja...  6.21 us

profile of v1, /device:TPU:0, one launch (start us, length us, event | category | flops | bytes accessed | tf_op | source)
XLA Modules:
  0.0 185.4 jit_solution(16433909809316974495)
XLA Ops:
  1.3 177.7 %shard_map.195 = (f32[1,512]{1,0:T(1,128)}, f32[512,2,256]{2,1,0:T(2,128)}, f32[1,2]{1,0:T(1,128)}, f32[1,256]{1,0:T(1,128)}, f32[2,80,256]{2,1,0:T(8,128)}, /*i...) custom-call(f32[512,2,256]{2,1,0:T(2,128)} %x_ref.1, ...), custom_call_target="tpu_custom_call" | custom-call | tf_op jit(solution)/shard_map/pallas_call | solution.py:1167
  179.0 6.2 %shard_map.196 = (f32[1,512]{1,0:T(1,128)}, f32[512,2,256]{2,1,0:T(2,128)}, f32[1,2]{1,0:T(1,128)}, f32[1,256]{1,0:T(1,128)}, f32[2,80,256]{2,1,0:T(8,128)}, /*i...) custom-call(f32[1,128]{1,0:T(1,128)} %get-tuple-element.31.scale_ref, ...), custom_call_target="tpu_custom_call" | custom-call | tf_op jit(solution)/shard_map/pallas_call | solution.py:1270

commit v2 on v1

--- a/solution.py
+++ b/solution.py
@@ -98,7 +98,7 @@
     return jnp.concatenate([v] * SEL, axis=0)
 
 
-def gate_state(c, groups):
+def gate_state(c, groups, swapped):
     w = SEL * groups
     zs = [c[w * b : w * b + w] * STEP_SLOPE for b in range(BITS)]
     alpha = c[w * BITS : w * BITS + w]
@@ -112,6 +112,8 @@
         small = e * big
         sig_p.append(jnp.where(z >= 0.0, big, small))
         sig_n.append(jnp.where(z >= 0.0, small, big))
+    last_on, last_off = ups[3], downs[3]
+    ups[3], downs[3] = jnp.where(swapped, last_off, last_on), jnp.where(swapped, last_on, last_off)
     low = [(ups[0] if k & 1 else downs[0]) + (ups[1] if k & 2 else downs[1]) for k in range(4)]
     high = [(ups[2] if k & 1 else downs[2]) + (ups[3] if k & 2 else downs[3]) for k in range(4)]
     log_r = [low[j & 3] + high[j >> 2] for j in range(E)]
@@ -121,33 +123,39 @@
     return log_r, r, mix, sig_p, sig_n
 
 
-def gate_forward(c, groups):
-    _, r, mix, _, _ = gate_state(c, groups)
+def gate_forward(c, groups, swapped):
+    _, r, mix, _, _ = gate_state(c, groups, swapped)
     return [over_selectors(mix * v, groups, jnp.add) for v in r]
 
 
-def gate_backward(c, dgate, groups, out):
-    log_r, r, mix, sig_p, sig_n = gate_state(c, groups)
-    yield
-    total = jnp.zeros_like(mix)
-    on = [jnp.zeros_like(mix) for _ in range(BITS)]
-    off = [jnp.zeros_like(mix) for _ in range(BITS)]
-    for j in range(E):
-        dg = to_selectors(dgate(j))
-        total = total + dg * r[j]
-        dlog = r[j] * (mix * dg - ENTROPY_WEIGHT * (log_r[j] + 1.0))
+class GateBackward:
+    def __init__(self, c, groups, swapped):
+        self.log_r, self.r, self.mix, self.sig_p, self.sig_n = gate_state(c, groups, swapped)
+        self.swapped = swapped
+        self.groups = groups
+        self.total = jnp.zeros_like(self.mix)
+        self.on = [jnp.zeros_like(self.mix) for _ in range(BITS)]
+        self.off = [jnp.zeros_like(self.mix) for _ in range(BITS)]
+
+    def add(self, j, dg):
+        dg = to_selectors(dg)
+        self.total = self.total + dg * self.r[j]
+        dlog = self.r[j] * (self.mix * dg - ENTROPY_WEIGHT * (self.log_r[j] + 1.0))
         for b in range(BITS):
             if j >> b & 1:
-                on[b] = on[b] + dlog
+                self.on[b] = self.on[b] + dlog
             else:
-                off[b] = off[b] + dlog
-        yield
-    dalpha = mix * (total - to_selectors(over_selectors(mix * total, groups, jnp.add)))
-    dz = [STEP_SLOPE * (on[b] * sig_n[b] - off[b] * sig_p[b]) for b in range(BITS)]
-    used = SEL * (BITS + 1) * groups
-    pad = jnp.zeros(((-used) % GROWS, c.shape[1]), F32)
-    out.append(jnp.concatenate(dz + [dalpha, pad], axis=0))
-    yield
+                self.off[b] = self.off[b] + dlog
+
+    def result(self):
+        mix, groups = self.mix, self.groups
+        dalpha = mix * (self.total - to_selectors(over_selectors(mix * self.total, groups, jnp.add)))
+        on, off = self.on[3], self.off[3]
+        self.on[3], self.off[3] = jnp.where(self.swapped, off, on), jnp.where(self.swapped, on, off)
+        dz = [STEP_SLOPE * (self.on[b] * self.sig_n[b] - self.off[b] * self.sig_p[b]) for b in range(BITS)]
+        used = SEL * (BITS + 1) * groups
+        pad = jnp.zeros(((-used) % GROWS, mix.shape[1]), F32)
+        return jnp.concatenate(dz + [dalpha, pad], axis=0)
 
 
 def t_dot(a, b):
@@ -156,7 +164,7 @@
     return lax.dot_general(left, tall(b), (((0,), (0,)), ((), ())), preferred_element_type=F32)
 
 
-def weave(count, first, middle, last, extra=()):
+def weave(count, first, middle, last, extra=(), after=None):
     extra = iter(extra)
     for step in range(count + 2):
         if step < count:
@@ -170,6 +178,8 @@
         next(extra, None)
         if 0 <= step - 1 < count:
             middle(step - 1, (step - 1) % 2, 1)
+            if after is not None:
+                after(step - 1)
         next(extra, None)
     for _ in extra:
         pass
@@ -253,6 +263,10 @@
     cs_next,
     acc_b,
     dy_kept,
+    tower_t,
+    tower_n,
+    out_cols,
+    dcs,
     held,
     tm,
     sb,
@@ -265,6 +279,7 @@
     local,
     fetch_sem,
     ready,
+    turns,
     rs_send,
     rs_recv,
     ag_send,
@@ -307,7 +322,9 @@
     fields = [pltpu.make_async_copy(x_ref.at[:, f], xf.at[f], local.at[2 + f]) for f in range(2)]
     for f in fields:
         f.start()
-    own = pl.ds(pl.multiple_of(c * HALF * H, HALF * H), HALF * H)
+    own = pl.ds(0, HALF * H)
+    mates = pl.ds(HALF * H, HALF * H)
+    swapped = c == 1
     own_in = pltpu.make_async_copy(win_ref, d_in.at[own], local.at[0])
     own_out = pltpu.make_async_copy(wout_ref, d_out.at[own], local.at[1])
     own_in.start()
@@ -332,8 +349,8 @@
     part[...] = xf[0] * fw_ref[0, 0] + xf[1] * fw_ref[0, 1]
     to_mate = copy(part.at[theirs], pre0, K_P, mate)
     to_mate.start()
-    swap_in = copy(win_ref, d_in.at[own], K_W, mate)
-    swap_out = copy(wout_ref, d_out.at[own], K_W + 1, mate)
+    swap_in = copy(win_ref, d_in.at[mates], K_W, mate)
+    swap_out = copy(wout_ref, d_out.at[mates], K_W + 1, mate)
     swap_in.start()
     swap_out.start()
     own_in.wait()
@@ -398,12 +415,12 @@
         put(wt.at[E + e], (slice(None),), d_out[expert(e)].T)
         return carry
 
-    lax.fori_loop(c * HALF, c * HALF + HALF, keep_plain, 0)
+    lax.fori_loop(0, HALF, keep_plain, 0)
 
     def keep_mates():
         swap_in.wait()
         swap_out.wait()
-        lax.fori_loop((1 - c) * HALF, (1 - c) * HALF + HALF, keep_plain, 0)
+        lax.fori_loop(HALF, E, keep_plain, 0)
 
     def rows_of(size):
         return [slice(a, a + TILE) for a in range(0, size, TILE)]
@@ -453,7 +470,7 @@
         )
 
     def give(e):
-        j = (1 - c) * HALF + e
+        j = HALF + e
         return (
             copy(d_in.at[expert(j)], rd.at[0, expert(e)], K_DX + e, mate),
             copy(d_out.at[expert(j)], rd.at[1, expert(e)], K_DX + HALF + e, mate),
@@ -466,7 +483,7 @@
 
     def turn_of(i):
         own_turn = i % 2
-        return ((1 - own_turn) * (1 - c) + own_turn * c) * HALF + near(i // 2)
+        return (1 - own_turn) * HALF + near(i // 2)
 
     def fetch(i):
         at = pl.ds((i % (AHEAD + 1)) * 8, 2 * SPILL)
@@ -488,8 +505,8 @@
         for move in give(e):
             move.wait_recv()
         rows = expert(e)
-        rd[0, rows] = (rd[0, rows] + d_in[expert(c * HALF + e)]).T
-        rd[1, rows] += d_out[expert(c * HALF + e)]
+        rd[0, rows] = (rd[0, rows] + d_in[rows]).T
+        rd[1, rows] += d_out[rows]
         return carry
 
     def ring_start():
@@ -516,12 +533,9 @@
         u_t[...] = tall(pooled.T)
         logits = mm(wide(wg[:FROWS]), u_t[...])
         cs[...] = logits
-        gates = gate_forward(logits, TASKS)
+        gates = gate_forward(logits, TASKS, swapped)
         for j, g in enumerate(gates):
             gt0[j] = g
-
-        def rows_at(j, tile):
-            return pl.ds(pl.multiple_of(j * H + tile.start, TILE), TILE)
 
         def forward(base):
             def first(i, par):
@@ -531,8 +545,8 @@
             def activate(i, par, part_no):
                 for tile in halves(R)[part_no]:
                     value, slope = gelu_pair(bb[par, tile])
-                    a1[rows_at(base + i, tile)] = value
-                    a2[rows_at(base + i, tile)] = slope
+                    a1[shifted(tile, base + i)] = value
+                    a2[shifted(tile, base + i)] = slope
                     put(gbuf, (base + i, tile), value)
 
             def finish(i, par):
@@ -540,9 +554,9 @@
 
             weave(HALF, first, activate, finish)
 
-        forward(c * HALF)
+        forward(0)
         keep_mates()
-        forward((1 - c) * HALF)
+        forward(HALF)
         columns[...] = jnp.concatenate(gates, axis=0).T
 
         for t in range(TASKS):
@@ -558,6 +572,28 @@
                 return carry
 
             lax.fori_loop(0, R // TILE, mix, 0)
+
+            @pl.when(c == 0)
+            def _():
+                if t == 0:
+                    copy(outbox.at[t], inbox.at[t], K_UP + t, across).start()
+
+        first_up = copy(outbox.at[0], inbox.at[0], K_UP, across)
+
+        @pl.when(c == 0)
+        def _():
+            first_up.wait_send()
+            pl.semaphore_signal(turns, inc=1, device_id={"section": mate}, device_id_type=MESH)
+            pl.semaphore_wait(turns, 1)
+
+        @pl.when(c == 1)
+        def _():
+            pl.semaphore_wait(turns, 1)
+            first_up.start()
+            first_up.wait_send()
+            pl.semaphore_signal(turns, inc=1, device_id={"section": mate}, device_id_type=MESH)
+
+        for t in range(1, TASKS):
             copy(outbox.at[t], inbox.at[t], K_UP + t, across).start()
 
         def flip(j, carry):
@@ -614,7 +650,7 @@
             yield
             u_n[t] = tall(inbox[t])
             yield
-            _, r, mix, _, _ = gate_state(logits, 1)
+            _, r, mix, _, _ = gate_state(logits, 1, swapped)
             yield
             for j in range(E):
                 gt_next[j] = over_selectors(mix * r[j], 1, jnp.add)
@@ -623,24 +659,16 @@
         def turn():
             u_t[...] = u_next[...]
             gt[...] = gt_next[...]
-            cs[GROWS : 2 * GROWS] = cs[:GROWS]
             cs[:GROWS] = cs_next[...]
-
-        def leave(t, at):
-            out = []
-            yield from gate_backward(cs[at : at + GROWS], lambda j: dgt[j, 0:1], 1, out)
-            outbox[t] = acc_b[...] + t_dot(wg[gate_rows(t)], out[0])
-            yield
-            dg[gate_rows(t)] = mm(wide(out[0]), u_n[t])
-            yield
 
         def all_of(pieces):
             for _ in pieces:
                 pass
 
-        cs[...] = jnp.zeros_like(cs)
-        dgt[...] = jnp.zeros_like(dgt)
-        acc_b[...] = jnp.zeros_like(acc_b)
+        for q in range(TASKS):
+            tower_t[q] = wide(ti[q].T)
+            tower_n[q] = wide(ti[q])
+            out_cols[q] = jnp.broadcast_to(sm[q][:, :TOWER].T[:, 2:3], (TOWER, R))
         copy(outbox.at[0], inbox.at[0], K_UP, across).wait_recv()
         all_of(enter(0))
         turn()
@@ -663,26 +691,19 @@
             def finish(j, par):
                 acc[...] += mm(pair(wt[E + j]), stack(gbuf[j]))
 
-            before = (t + TASKS - 1) % TASKS
-            weave(E, first, activate, finish, leave(before, GROWS))
+            weave(E, first, activate, finish)
             keep_start(0, t)
-
-            @pl.when(t > 0)
-            def _():
-                copy(outbox.at[before], inbox.at[before], K_DOWN + before, across).start()
 
             second = acc[...]
             held[...] = second
-            tower = ti[t]
-            g, slope = gelu_pair(mm(wide(tower.T), tall(second)))
-            info = sm[t]
-            out_col = info[:, :TOWER].T[:, 2:3]
+            g, slope = gelu_pair(mm(tower_t[t], tall(second)))
+            out_col = out_cols[t]
             here = sm[t, :, mine]
             logit = jnp.sum(g * out_col, axis=0, keepdims=True) + here[3:4]
             prob = jax.nn.sigmoid(logit)
             dlogit = here[1:2] * (prob - here[0:1])
             m = dlogit * out_col * slope
-            dy = mm(wide(tower), tall(m))
+            dy = mm(tower_n[t], tall(m))
             s_t[...] = tall(dy)
             acc_b[...] = dy
             dy_kept[...] = dy
@@ -738,7 +759,12 @@
                 tp[t, TOWER + 1 : TOWER + 2] = jnp.concatenate([out_row, jnp.zeros_like(out_row)], axis=1)
                 yield
 
-            weave(E, back, pull, spread, beside())
+            gates_back = GateBackward(cs[:GROWS], 1, swapped)
+            weave(E, back, pull, spread, beside(), lambda j: gates_back.add(j, dgt[j, 0:1]))
+            dc = gates_back.result()
+            outbox[t] = acc_b[...] + t_dot(wg[gate_rows(t)], dc)
+            copy(outbox.at[t], inbox.at[t], K_DOWN + t, across).start()
+            dcs[gate_rows(t)] = dc
             keep_start(1, t)
             turn()
 
@@ -753,9 +779,9 @@
             return carry
 
         lax.fori_loop(0, TASKS, task, 0)
-        last_task = TASKS - 1
-        all_of(leave(last_task, GROWS))
-        copy(outbox.at[last_task], inbox.at[last_task], K_DOWN + last_task, across).start()
+        for q in range(TASKS):
+            rows = slice(q * GROWS, (q + 1) * GROWS)
+            dg[rows] = mm(wide(dcs[rows]), u_n[q])
         greet_ring()
 
     @pl.when(x == 1)
@@ -884,10 +910,10 @@
 
     @pl.when(x == 0)
     def _():
-        out = []
-        for _ in gate_backward(cs[...], lambda j: dgt[j, :TASKS], TASKS, out):
-            pass
-        dc = out[0]
+        gates_back = GateBackward(cs[...], TASKS, swapped)
+        for j in range(E):
+            gates_back.add(j, dgt[j, :TASKS])
+        dc = gates_back.result()
         dpool = (acc[...] + t_dot(wg[:FROWS], dc)).T
         pre_rows = pre[...]
         rho = lax.rsqrt(jnp.mean(pre_rows * pre_rows, axis=1, keepdims=True) + NORM_EPS)
@@ -1084,7 +1110,7 @@
 
     @pl.when(x == 0)
     def _():
-        for t in range(TASKS):
+        for t in range(1, TASKS):
             copy(outbox.at[t], inbox.at[t], K_UP + t, across).wait_send()
         for k, sec in enumerate((mate, across, diag)):
             copy(dp.at[mine], dp.at[mine], K_DP + c, sec, K_DP + k).wait_send()
@@ -1228,6 +1254,10 @@
             f32(GROWS, half),
             f32(D, half),
             f32(D, half),
+            bf(TASKS, TOWER, 3 * D),
+            bf(TASKS, D, 3 * TOWER),
+            f32(TASKS, TOWER, half),
+            f32(TASKS * GROWS, half),
             f32(D, half),
             f32(2 * TOWER, half),
             f32(n * small_rows, D),
@@ -1239,6 +1269,7 @@
             dma((K_COUNT,)),
             dma((6,)),
             dma((AHEAD + 1,)),
+            pltpu.SemaphoreType.REGULAR,
             pltpu.SemaphoreType.REGULAR,
             dma((2, subs, n - 1)),
             dma((2, subs, n - 1)),

time: 186 us -> 186 us (level)
  no operation moved by 1% of the time
where the time goes in v2:
time: 186 us; the launch traced here: 185 us
  Pallas kernels  184 us (99%)
    pallas_call x1, Pallas kernels, body(): pl.pallas_call(partial(kernel, n, subs, small_rows), out_shape=(out(1, ro...  178 us
    pallas_call x1, Pallas kernels, body(): pl.pallas_call(partial(hand_over, len(sums), (5, 6)), out_shape=tuple((ja...  6.21 us

profile of v2, /device:TPU:0, one launch (start us, length us, event | category | flops | bytes accessed | tf_op | source)
XLA Modules:
  0.0 185.4 jit_solution(7824407375270363655)
XLA Ops:
  1.3 177.7 %shard_map.195 = (f32[1,512]{1,0:T(1,128)}, f32[512,2,256]{2,1,0:T(2,128)}, f32[1,2]{1,0:T(1,128)}, f32[1,256]{1,0:T(1,128)}, f32[2,80,256]{2,1,0:T(8,128)}, /*i...) custom-call(f32[512,2,256]{2,1,0:T(2,128)} %x_ref.1, ...), custom_call_target="tpu_custom_call" | custom-call | tf_op jit(solution)/shard_map/pallas_call | solution.py:1193
  179.0 6.2 %shard_map.196 = (f32[1,512]{1,0:T(1,128)}, f32[512,2,256]{2,1,0:T(2,128)}, f32[1,2]{1,0:T(1,128)}, f32[1,256]{1,0:T(1,128)}, f32[2,80,256]{2,1,0:T(8,128)}, /*i...) custom-call(f32[1,128]{1,0:T(1,128)} %get-tuple-element.31.scale_ref, ...), custom_call_target="tpu_custom_call" | custom-call | tf_op jit(solution)/shard_map/pallas_call | solution.py:1301

commit v3 on v0

--- a/solution.py
+++ b/solution.py
@@ -550,9 +550,7 @@
             copy(outbox.at[t], inbox.at[t], K_UP + t, across).start()
 
         def flip(j, carry):
-            value = a1[expert(j)].T
-            a1[expert(j)] = value
-            put(gbuf.at[j], (slice(None),), value)
+            put(gbuf.at[j], (slice(None),), a1[expert(j)].T)
             a2[expert(j)] = a2[expert(j)].T
             d_in[expert(j)] = d_in[expert(j)].T
             return carry

time: 185 us -> 185 us (level)
  no operation moved by 1% of the time
where the time goes in v3:
time: 185 us
  Pallas kernels  184 us (99%)
    pallas_call x1, Pallas kernels, body(): pl.pallas_call(partial(kernel, n, subs, small_rows), out_shape=(out(1, ro...  178 us
    pallas_call x1, Pallas kernels, body(): pl.pallas_call(partial(hand_over, len(sums)), out_shape=tuple((jax.ShapeD...  5.44 us

profile of v3, /device:TPU:0, one launch (start us, length us, event | category | flops | bytes accessed | tf_op | source)
XLA Modules:
  0.0 185.0 jit_solution(2196149985553597809)
XLA Ops:
  1.3 178.1 %shard_map.195 = (f32[1,512]{1,0:T(1,128)}, f32[512,2,256]{2,1,0:T(2,128)}, f32[1,2]{1,0:T(1,128)}, f32[1,256]{1,0:T(1,128)}, f32[2,80,256]{2,1,0:T(8,128)}, /*i...) custom-call(f32[512,2,256]{2,1,0:T(2,128)} %x_ref.1, ...), custom_call_target="tpu_custom_call" | custom-call | tf_op jit(solution)/shard_map/pallas_call | solution.py:1138
  179.4 5.4 %shard_map.196 = (f32[1,512]{1,0:T(1,128)}, f32[512,2,256]{2,1,0:T(2,128)}, f32[1,2]{1,0:T(1,128)}, f32[1,256]{1,0:T(1,128)}, f32[2,80,256]{2,1,0:T(8,128)}, /*i...) custom-call(f32[1,512]{1,0:T(1,128)} %get-tuple-element.30.refs_0_, ...), custom_call_target="tpu_custom_call" | custom-call | tf_op jit(solution)/shard_map/pallas_call | solution.py:1240
